TPU v7x, 32 devices: a whole 2x2x4 slice. The times are simulated.
32 devices in a mesh: ctx: 32 (over z, y, x, core), ch: 1.
Axes of the slice: x: 2, y: 2, z: 4, core: 2. Of those that a mesh axis runs over, the one named last changes fastest.
Arguments:
- query_branch: bfloat16 [8192, 2048], P('ctx', 'ch'), may hold values from -6 to 6
- key_branch: bfloat16 [8192, 2048], P('ctx', 'ch'), may hold values from -6 to 6
- value_branch: bfloat16 [8192, 2048], P('ctx', 'ch'), may hold values from -6 to 6
- grad_output: bfloat16 [8192, 2048], P('ctx', 'ch'), may hold values from -6 to 6
- conv_output: bfloat16 [8192, 2048], P('ctx', 'ch'), may hold values from -6 to 6
- filters: float32 [8192, 512], P('ctx'), may hold values from -0.09375 to 0.09375
- genome_blocks: int32 [4], replicated, may hold values from 1 to 16, 32 in all
Outputs:
- grad_query: bfloat16 [8192, 2048], P('ctx', 'ch')
- grad_key: bfloat16 [8192, 2048], P('ctx', 'ch')
- grad_value: bfloat16 [8192, 2048], P('ctx', 'ch')
- grad_filters: float32 [8192, 512], P('ctx', 'ch')
Inputs may be any that keep to these rules, and one draw needn't show every extreme that they name: `genome_blocks`: the genomes lie in order and fill the row; the longest covers exactly 16 shards.
All inputs are finite; a program needn't handle non-finite values.
Results may differ from a plain program's by a relative error of at most 0.001.
Values sent between devices are 32-bit elements; how exact they have to be, the bound alone decides.
A program may use at most 128 MiB of HBM per device.

v0:
```python
import math

import jax
import jax.numpy as jnp
from jax import lax
from jax.sharding import PartitionSpec as P

HIGH = lax.Precision.HIGHEST


def dft_tables(length):
    freq = jnp.arange(length, dtype=jnp.int32)
    sample = jnp.arange(2 * length, dtype=jnp.int32)
    phase = freq[:, None] * sample[None, :] % (2 * length)
    angle = phase.astype(jnp.float32) * (math.pi / length)
    parity = (1 - 2 * (sample % 2)).astype(jnp.float32)
    first = (freq == 0)[:, None]
    fwd_real = jnp.cos(angle)
    fwd_imag = jnp.where(first, parity[None, :], -jnp.sin(angle))
    inv_real = (jnp.where(first, 1.0, 2.0) * jnp.cos(angle)).T / (2 * length)
    inv_imag = jnp.where(first, parity[None, :], -2.0 * jnp.sin(angle)).T / (2 * length)
    return (fwd_real, fwd_imag, inv_real, inv_imag)


def transform(signal, real_table, imag_table):
    real = jnp.dot(real_table, signal, precision=HIGH, preferred_element_type=jnp.float32)
    imag = jnp.dot(imag_table, signal, precision=HIGH, preferred_element_type=jnp.float32)
    return jnp.stack([real, imag], axis=0)[None]


def inverse(spectrum, real_table, imag_table):
    real = jnp.dot(real_table, spectrum[0], precision=HIGH, preferred_element_type=jnp.float32)
    return real + jnp.dot(
        imag_table, spectrum[1], precision=HIGH, preferred_element_type=jnp.float32
    )


def conj_product(first, second, zero_row):
    a_re = first[..., 0, :, :]
    a_im = first[..., 1, :, :]
    b_re = second[..., 0, :, :]
    b_im = second[..., 1, :, :]
    real = jnp.where(zero_row, a_re * b_re, a_re * b_re + a_im * b_im)
    imag = jnp.where(zero_row, a_im * b_im, a_re * b_im - a_im * b_re)
    return jnp.stack([real, imag], axis=-3)


def lag_sweep(gated_blk, carried_blk, filter_blk, block_ids, zero_row, repeats, width, blocks):
    lag_cap = blocks // 2
    group = 8
    padded_ids = jnp.concatenate([block_ids, jnp.full((blocks,), -1, jnp.int32)])
    padded_carried = jnp.concatenate([carried_blk, jnp.zeros_like(carried_blk)], axis=0)
    freqs = carried_blk.shape[2]

    def lag_group(step, state):
        accum, lag_grads = state
        for sub in range(group):
            lag = step * group + sub
            later = lax.dynamic_slice_in_dim(padded_carried, lag, blocks, 0)
            same = lax.dynamic_slice_in_dim(padded_ids, lag, blocks, 0) == block_ids
            weight = same.astype(jnp.float32)[:, None, None, None]
            kernel = lax.dynamic_index_in_dim(filter_blk, lag, 0, keepdims=False)
            kernel = jnp.tile(kernel, (1, 1, repeats))
            accum = accum + weight * conj_product(kernel, later, zero_row)
            term = jnp.sum(weight * conj_product(gated_blk, later, zero_row), axis=0)
            term = term.reshape(2, freqs, repeats, width).sum(axis=2)
            lag_grads = lax.dynamic_update_index_in_dim(lag_grads, term, lag, 0)
        return (accum, lag_grads)

    start_state = (jnp.zeros_like(carried_blk), jnp.zeros((blocks, 2, freqs, width), jnp.float32))
    return lax.fori_loop(0, lag_cap // group, lag_group, start_state)


def local(query_branch, key_branch, value_branch, grad_output, conv_output, filters, genome_blocks):
    rows, channels = query_branch.shape
    width = filters.shape[1]
    repeats = channels // width
    blocks = lax.axis_size("ctx")
    here = lax.axis_index("ctx")
    slab = rows // blocks
    query32 = query_branch.astype(jnp.float32)
    key32 = key_branch.astype(jnp.float32)
    gated = query32 * key32
    carried = grad_output.astype(jnp.float32) * value_branch.astype(jnp.float32)
    grad_value = (grad_output.astype(jnp.float32) * conv_output.astype(jnp.float32)).astype(
        jnp.bfloat16
    )
    fwd_real, fwd_imag, inv_real, inv_imag = dft_tables(rows)
    ends = jnp.cumsum(genome_blocks)
    block_ids = jnp.sum(
        (ends[None, :] <= jnp.arange(blocks, dtype=jnp.int32)[:, None]).astype(jnp.int32), axis=1
    )
    scale = (rows * blocks) ** (-0.5)
    summed = False
    gated_spec = transform(gated, fwd_real[:, :rows], fwd_imag[:, :rows])
    carried_spec = transform(carried, fwd_real[:, :rows], fwd_imag[:, :rows])
    filter_spec = transform(filters, fwd_real[:, :rows], fwd_imag[:, :rows])
    gated_blk, carried_blk, own_blk = (
        lax.all_to_all(gated_spec, "ctx", split_axis=2, concat_axis=0, tiled=True),
        lax.all_to_all(carried_spec, "ctx", split_axis=2, concat_axis=0, tiled=True),
        lax.all_to_all(filter_spec, "ctx", split_axis=2, concat_axis=0, tiled=True),
    )
    global_freq = here * slab + jnp.arange(slab, dtype=jnp.int32)
    zero_row = (global_freq == 0)[:, None]
    flip = jnp.where(zero_row, 1.0, (1 - 2 * (global_freq % 2)).astype(jnp.float32)[:, None])
    prior_blk = jnp.concatenate([jnp.zeros_like(own_blk[:1]), own_blk[:-1]], axis=0)
    filter_blk = own_blk + flip * prior_blk
    accum, lag_grads = lag_sweep(
        gated_blk, carried_blk, filter_blk, block_ids, zero_row, repeats, width, blocks
    )
    following = jnp.concatenate([lag_grads[1:], jnp.zeros_like(lag_grads[:1])], axis=0)
    lag_grads = lag_grads + flip * following
    back_carried, back_lags = (
        lax.all_to_all(accum, "ctx", split_axis=0, concat_axis=2, tiled=True),
        lax.all_to_all(lag_grads, "ctx", split_axis=0, concat_axis=2, tiled=True),
    )
    back = inverse(back_carried[0], inv_real[:rows], inv_imag[:rows])
    scaled = inverse(back_lags[0], inv_real[:rows], inv_imag[:rows]) * scale
    grad_query = (back * key32).astype(jnp.bfloat16)
    grad_key = (back * query32).astype(jnp.bfloat16)
    grad_filters = lax.psum_scatter(scaled, "ch", scatter_dimension=1, tiled=True)
    return (grad_query, grad_key, grad_value, grad_filters)


def solution(mesh):
    in_specs = (
        P("ctx", "ch"),
        P("ctx", "ch"),
        P("ctx", "ch"),
        P("ctx", "ch"),
        P("ctx", "ch"),
        P("ctx", None),
        P(),
    )
    out_specs = (P("ctx", "ch"), P("ctx", "ch"), P("ctx", "ch"), P("ctx", "ch"))
    return jax.shard_map(local, mesh=mesh, in_specs=in_specs, out_specs=out_specs, check_vma=False)
```

profile of v0, /device:TPU:0, one launch (start us, length us, event | category | flops | bytes accessed | tf_op | source)
XLA Modules:
  0.0 568.9 jit_solution(7487782737807145501)
XLA Ops:
  1.7 1.5 convolution_bitcast_fusion.5
  3.2 1.5 convolution_bitcast_fusion.4
  4.8 1.8 copy.20
  6.5 7.6 %all-to-all-start = ((f32[1,2,256,512]{3,1,0,2:T(2,128)}), f32[1,2,256,512]{3,1,0,2:T(2,128)}, u32[]{:S(2)}, u32[]{:S(2)}) async-start(f32[1,2,256,512]{3,1,0,2:T(2,128)} %copy.20), calls=%async_computation | async-start | bytes 2097152 | tf_op jit(solution)/shard_map/all_to_all | solution.py:101
  14.2 2.8 convolution_bitcast_fusion.3
  17.0 2.9 convolution_bitcast_fusion.2
  20.4 5.2 copy.22
  25.6 14.7 %all-to-all-done = f32[1,2,256,512]{3,1,0,2:T(2,128)} async-done(((f32[1,2,256,512]{3,1,0,2:T(2,128)}), f32[1,2,256,512]{3,1,0,2:T(2,128)}, u32[]{:S(2)}, u32[]{:S(2)}) %all-to-all-start) | async-done | bytes 1048608 | tf_op jit(solution)/shard_map/all_to_all | solution.py:101
  40.3 4.0 all-to-all-start.1
  44.3 2.8 convolution_bitcast_fusion.1
  47.2 2.9 convolution_bitcast_fusion
  50.6 5.2 copy.24
  55.8 82.4 %all-to-all-done.1 = f32[1,2,256,2048]{3,1,0,2:T(2,128)} async-done(((f32[1,2,256,2048]{3,1,0,2:T(2,128)}), f32[1,2,256,2048]{3,1,0,2:T(2,128)}, u32[]{:S(2)}, u32[]{:S(2)}) %all-to-all-start.1) | async-done | bytes 4194336 | tf_op jit(solution)/shard_map/all_to_all | solution.py:100
  138.2 4.5 all-to-all-start.2
  143.0 1.4 copy.32
  144.5 2.6 bitcast_add_fusion
  147.1 7.9 %copy.31 = f32[1,2,32,8,2048]{4,3,1,2,0:T(8,128)} copy(f32[1,2,32,8,2048]{4,1,3,2,0:T(2,128)} %bitcast.12) | data formatting | bytes 8388608 | tf_op jit(solution)/shard_map/all_to_all | solution.py:100
  155.0 81.6 %all-to-all-done.2 = f32[1,2,256,2048]{3,1,0,2:T(2,128)} async-done(((f32[1,2,256,2048]{3,1,0,2:T(2,128)}), f32[1,2,256,2048]{3,1,0,2:T(2,128)}, u32[]{:S(2)}, u32[]{:S(2)}) %all-to-all-start.2) | async-done | bytes 4194336 | tf_op jit(solution)/shard_map/all_to_all | solution.py:99
  236.6 8.1 %copy.30 = f32[1,2,32,8,2048]{4,3,1,2,0:T(8,128)} copy(f32[1,2,32,8,2048]{4,1,3,2,0:T(2,128)} %bitcast.18) | data formatting | bytes 8388608 | tf_op jit(solution)/shard_map/all_to_all | solution.py:99
  244.8 4.3 concatenate.14
  250.1 178.4 %while.18 = (s32[]{:T(128)}, f32[32,2,8,2048]{3,2,1,0:T(8,128)}, f32[32,2,8,512]{3,2,1,0:T(8,128)}, s32[64]{0:T(128)S(1)}, s32[32]{0:T(128)S(1)}, /*index=5*/f32...) while((s32[]{:T(128)}, f32[32,2,8,2048]{3,2,1,0:T(8,128)}, ...), condition=%wide.region_19.20_spmd.clone, body=%wide.region_2.19_spmd.clone.sunk | while | flops 119996992 | bytes 270013728 | solution.py:71
  251.4 13.1 %add_select_fusion.25 = (f32[32,1,8,2048]{3,2,1,0:T(8,128)}, f32[32,1,8,2048]{3,2,1,0:T(8,128)}, f32[32,1,8,2048]{3,2,1,0:T(8,128)}, f32[32,1,8,2048]{3,2,1,0:T(...) fusion(f32[64,2,8,2048]{3,2,1,0:T(8,128)} %get-tuple-element.63, ...), kind=kLoop, calls=%fused_computation.38.clone.1 | loop fusion | flops 17301504 | bytes 38010908 | tf_op jit(solution)/shard_map/while/body/eval_jaxpr/jit(_where)/select_n | solution.py:43
  264.5 12.5 %subtract_select_fusion.17 = (f32[32,1,8,2048]{3,2,1,0:T(8,128)}, f32[32,1,8,2048]{3,2,1,0:T(8,128)}, f32[32,1,8,2048]{3,2,1,0:T(8,128)}, f32[32,1,8,2048]{3,2,1...) fusion(f32[64,2,8,2048]{3,2,1,0:T(8,128)} %get-tuple-element.630, s32[]{:T(128)S(6)} %select_n.788, ...), kind=kLoop, calls=%fused_computation.49.clone.1 | loop fusion | flops 13107200 | bytes 33554460 | tf_op jit(solution)/shard_map/while/body/eval_jaxpr/jit(_where)/select_n | solution.py:44
  277.1 3.9 fusion.78
  282.3 11.6 %add_select_fusion.26 = (f32[32,1,8,2048]{3,2,1,0:T(8,128)}, f32[32,1,8,2048]{3,2,1,0:T(8,128)S(1)}, f32[32,1,8,2048]{3,2,1,0:T(8,128)S(1)}, f32[32,1,8,2048]{3,...) fusion(f32[64,2,8,2048]{3,2,1,0:T(8,128)} %get-tuple-element.630, s32[]{:T(128)S(6)} %select_n.788, ...), kind=kLoop, calls=%fused_computation.33.clone.1 | loop fusion | flops 13107200 | bytes 33554460 | tf_op jit(solution)/shard_map/while/body/eval_jaxpr/jit(_where)/select_n | solution.py:43
  296.1 3.9 fusion.80
  301.3 3.9 fusion.81
  306.6 15.6 %add_select_fusion.24 = (f32[32,1,8,2048]{3,2,1,0:T(8,128)}, f32[32,1,8,2048]{3,2,1,0:T(8,128)}, f32[32,1,8,2048]{3,2,1,0:T(8,128)}, f32[32,1,8,2048]{3,2,1,0:T(...) fusion(f32[64,2,8,2048]{3,2,1,0:T(8,128)} %get-tuple-element.63, ...), kind=kLoop, calls=%fused_computation.42.clone.1 | loop fusion | flops 20971520 | bytes 42598432 | tf_op jit(solution)/shard_map/while/body/eval_jaxpr/jit(_where)/select_n | solution.py:43
  322.3 3.0 add_select_fusion.23
  325.2 13.2 %fusion.77 = f32[32,2,8,2048]{3,2,1,0:T(8,128)} fusion(f32[32,1,8,2048]{3,2,1,0:T(8,128)} %get-tuple-element.490, f32[32,1,8,2048]{3,2,1,0:T(8,128)} %get-tuple-element.491, f32[32,1,8,2048]{3,2,1,0:T(8,128)} %get-tuple-element.502, f32[32,1,8,2048]{3,2,1,0:T(8,128)} %get-tuple-element.503, f32[32,1,8,2048]{3,2,1,0:T(8,128)} %get-tuple-element.508, ...), kind=kLoop, calls=%fused_computation.9.clone.1 | loop fusion | flops 26214400 | bytes 41944064 | tf_op jit(solution)/shard_map/while/body/eval_jaxpr/add | solution.py:64
  339.5 13.1 %add_select_fusion.25 = (f32[32,1,8,2048]{3,2,1,0:T(8,128)}, f32[32,1,8,2048]{3,2,1,0:T(8,128)}, f32[32,1,8,2048]{3,2,1,0:T(8,128)}, f32[32,1,8,2048]{3,2,1,0:T(...) fusion(f32[64,2,8,2048]{3,2,1,0:T(8,128)} %get-tuple-element.63, ...), kind=kLoop, calls=%fused_computation.38.clone.1 | loop fusion | flops 17301504 | bytes 38010908 | tf_op jit(solution)/shard_map/while/body/eval_jaxpr/jit(_where)/select_n | solution.py:43
  352.7 12.7 %subtract_select_fusion.17 = (f32[32,1,8,2048]{3,2,1,0:T(8,128)}, f32[32,1,8,2048]{3,2,1,0:T(8,128)}, f32[32,1,8,2048]{3,2,1,0:T(8,128)}, f32[32,1,8,2048]{3,2,1...) fusion(f32[64,2,8,2048]{3,2,1,0:T(8,128)} %get-tuple-element.630, s32[]{:T(128)S(6)} %select_n.788, ...), kind=kLoop, calls=%fused_computation.49.clone.1 | loop fusion | flops 13107200 | bytes 33554460 | tf_op jit(solution)/shard_map/while/body/eval_jaxpr/jit(_where)/select_n | solution.py:44
  365.4 3.9 fusion.78
  370.6 11.6 %add_select_fusion.26 = (f32[32,1,8,2048]{3,2,1,0:T(8,128)}, f32[32,1,8,2048]{3,2,1,0:T(8,128)S(1)}, f32[32,1,8,2048]{3,2,1,0:T(8,128)S(1)}, f32[32,1,8,2048]{3,...) fusion(f32[64,2,8,2048]{3,2,1,0:T(8,128)} %get-tuple-element.630, s32[]{:T(128)S(6)} %select_n.788, ...), kind=kLoop, calls=%fused_computation.33.clone.1 | loop fusion | flops 13107200 | bytes 33554460 | tf_op jit(solution)/shard_map/while/body/eval_jaxpr/jit(_where)/select_n | solution.py:43
  384.5 3.9 fusion.80
  389.7 3.9 fusion.81
  395.0 15.5 %add_select_fusion.24 = (f32[32,1,8,2048]{3,2,1,0:T(8,128)}, f32[32,1,8,2048]{3,2,1,0:T(8,128)}, f32[32,1,8,2048]{3,2,1,0:T(8,128)}, f32[32,1,8,2048]{3,2,1,0:T(...) fusion(f32[64,2,8,2048]{3,2,1,0:T(8,128)} %get-tuple-element.63, ...), kind=kLoop, calls=%fused_computation.42.clone.1 | loop fusion | flops 20971520 | bytes 42598432 | tf_op jit(solution)/shard_map/while/body/eval_jaxpr/jit(_where)/select_n | solution.py:43
  410.6 3.0 add_select_fusion.23
  413.6 14.7 %fusion.77 = f32[32,2,8,2048]{3,2,1,0:T(8,128)} fusion(f32[32,1,8,2048]{3,2,1,0:T(8,128)} %get-tuple-element.490, f32[32,1,8,2048]{3,2,1,0:T(8,128)} %get-tuple-element.491, f32[32,1,8,2048]{3,2,1,0:T(8,128)} %get-tuple-element.502, f32[32,1,8,2048]{3,2,1,0:T(8,128)} %get-tuple-element.503, f32[32,1,8,2048]{3,2,1,0:T(8,128)} %get-tuple-element.508, ...), kind=kLoop, calls=%fused_computation.9.clone.1 | loop fusion | flops 26214400 | bytes 41944064 | tf_op jit(solution)/shard_map/while/body/eval_jaxpr/add | solution.py:64
  428.5 1.4 slice.513
  430.4 30.0 %all_to_all.84 = f32[32,2,8,512]{3,2,1,0:T(8,128)S(1)} all-to-all(f32[32,2,8,512]{3,2,1,0:T(8,128)S(1)} %multiply_add_fusion), channel_id=1, replica_groups=mesh['ctx'=32,'ch'=1] {'ctx'}, dimensions={0} | all-to-all | bytes 2097152 | tf_op jit(solution)/shard_map/all_to_all | solution.py:115
  460.4 3.7 all-to-all-start.3
  464.4 2.6 fusion.18
  467.0 1.5 fusion.29
  468.5 2.3 fusion.22
  470.8 87.2 %all-to-all-done.3 = f32[32,2,8,2048]{3,2,1,0:T(8,128)} async-done(((f32[32,2,8,2048]{3,2,1,0:T(8,128)}), f32[32,2,8,2048]{3,2,1,0:T(8,128)}, u32[]{:S(2)}, u32[]{:S(2)}) %all-to-all-start.3) | async-done | bytes 4194336 | tf_op jit(solution)/shard_map/all_to_all | solution.py:114
  558.0 4.5 fusion.21
  562.5 6.1 %fusion.19 = (bf16[256,2048]{1,0:T(8,128)(2,1)}, bf16[256,2048]{1,0:T(8,128)(2,1)}) fusion(bf16[256,2048]{1,0:T(8,128)(2,1)S(1)} %copy-done.7, bf16[256,2048]{1,0:T(8,128)(2,1)S(1)} %copy-done.9, f32[256,2048]{1,0:T(8,128)S(1)} %fusion.21, f32[1,2,32,8,2048]{4,3,1,2,0:T(8,128)} %bitcast.22, f32[512,256]{1,0:T(8,128)S(1)} %fusion.25, ...), kind=kOutput, calls=%fused_computation.121 | convolution fusion | flops 1614479360 | bytes 8652288 | tf_op jit(solution)/shard_map/dot_general | solution.py:33
  (139 shorter events, 18.7 us)
Async XLA Ops:
  0.6 1.1 copy-start
  0.9 46.3 %copy-start.14 = (pred[256]{0:T(512)(128)(4,1)}, pred[256]{0:T(512)(128)(4,1)S(1)}, u32[]{:S(2)}) copy-start(pred[256]{0:T(512)(128)(4,1)S(1)} %iota_compare_fusion.1) | copy-start | bytes 772
  1.7 45.5 %copy-start.12 = (f32[256]{0:T(256)}, f32[256]{0:T(256)S(1)}, u32[]{:S(2)}) copy-start(f32[256]{0:T(256)S(1)} %slice.569) | copy-start | bytes 3076
  4.7 9.4 %copy-start.4 = (bf16[256,2048]{1,0:T(8,128)(2,1)S(1)}, bf16[256,2048]{1,0:T(8,128)(2,1)}, u32[]{:S(2)}) copy-start(bf16[256,2048]{1,0:T(8,128)(2,1)} %param.12) | copy-start | bytes 3145732
  4.8 9.4 %copy-start.11 = (bf16[256,2048]{1,0:T(8,128)(2,1)S(1)}, bf16[256,2048]{1,0:T(8,128)(2,1)}, u32[]{:S(2)}) copy-start(bf16[256,2048]{1,0:T(8,128)(2,1)} %param.11) | copy-start | bytes 3145732
  6.5 33.8 %all-to-all-start = ((f32[1,2,256,512]{3,1,0,2:T(2,128)}), f32[1,2,256,512]{3,1,0,2:T(2,128)}, u32[]{:S(2)}, u32[]{:S(2)}) async-start(f32[1,2,256,512]{3,1,0,2:T(2,128)} %copy.20), calls=%async_computation | async-start | bytes 2097152 | tf_op jit(solution)/shard_map/all_to_all | solution.py:101
  25.6 18.7 %copy-start.6 = (bf16[256,2048]{1,0:T(8,128)(2,1)S(1)}, bf16[256,2048]{1,0:T(8,128)(2,1)}, u32[]{:S(2)}) copy-start(bf16[256,2048]{1,0:T(8,128)(2,1)} %param.9) | copy-start | bytes 3145732
  25.6 18.7 %copy-start.8 = (bf16[256,2048]{1,0:T(8,128)(2,1)S(1)}, bf16[256,2048]{1,0:T(8,128)(2,1)}, u32[]{:S(2)}) copy-start(bf16[256,2048]{1,0:T(8,128)(2,1)} %param.10) | copy-start | bytes 3145732
  40.3 97.9 %all-to-all-start.1 = ((f32[1,2,256,2048]{3,1,0,2:T(2,128)}), f32[1,2,256,2048]{3,1,0,2:T(2,128)}, u32[]{:S(2)}, u32[]{:S(2)}) async-start(f32[1,2,256,2048]{3,1,0,2:T(2,128)} %copy.22), calls=%async_computation.1 | async-start | bytes 8388608 | tf_op jit(solution)/shard_map/all_to_all | solution.py:100
  55.8 86.9 %copy-start.18 = (s32[4]{0:T(128)S(1)}, s32[4]{0:T(128)}, u32[]{:S(2)}) copy-start(s32[4]{0:T(128)} %param.15) | copy-start | bytes 52
  138.2 98.4 %all-to-all-start.2 = ((f32[1,2,256,2048]{3,1,0,2:T(2,128)}), f32[1,2,256,2048]{3,1,0,2:T(2,128)}, u32[]{:S(2)}, u32[]{:S(2)}) async-start(f32[1,2,256,2048]{3,1,0,2:T(2,128)} %copy.24), calls=%async_computation.2 | async-start | bytes 8388608 | tf_op jit(solution)/shard_map/all_to_all | solution.py:99
  143.0 4.1 copy-start.16
  236.6 8.1 %copy-start.3 = (f32[1,2,32,8,2048]{4,3,1,2,0:T(8,128)S(1)}, f32[1,2,32,8,2048]{4,3,1,2,0:T(8,128)}, u32[]{:S(2)}) copy-start(f32[1,2,32,8,2048]{4,3,1,2,0:T(8,128)} %copy.31) | copy-start | bytes 12582916
  250.1 179.8 %copy-start.17 = (f32[8]{0:T(128)S(1)}, f32[8]{0:T(128)}, u32[]{:S(2)}) copy-start(f32[8]{0:T(128)} %copy-done.16) | copy-start | bytes 100
  282.3 11.6 %copy-start.2 = (f32[32,1,8,2048]{3,2,1,0:T(8,128)S(1)}, f32[32,1,8,2048]{3,2,1,0:T(8,128)}, u32[]{:S(2)}) copy-start(f32[32,1,8,2048]{3,2,1,0:T(8,128)} %get-tuple-element.535) | copy-start | bytes 6291460 | tf_op jit(solution)/shard_map/while
  306.6 15.6 %slice-start = ((s8[8388608]{0:T(1024)(128)(4,1)}), s8[4194304]{0:T(1024)(128)(4,1)S(1)}, s32[]{:S(2)}) async-start(s8[8388608]{0:T(1024)(128)(4,1)} %bitcast.205), calls=%async_computation.5 | async-start | bytes 8388608 | tf_op jit(solution)/shard_map/while
  306.6 15.6 %slice-start.1 = ((s8[8388608]{0:T(1024)(128)(4,1)}), s8[4194304]{0:T(1024)(128)(4,1)S(1)}, s32[]{:S(2)}) async-start(s8[8388608]{0:T(1024)(128)(4,1)} %bitcast.205), calls=%async_computation.6 | async-start | bytes 8388608 | tf_op jit(solution)/shard_map/while
  370.6 11.6 %copy-start.2 = (f32[32,1,8,2048]{3,2,1,0:T(8,128)S(1)}, f32[32,1,8,2048]{3,2,1,0:T(8,128)}, u32[]{:S(2)}) copy-start(f32[32,1,8,2048]{3,2,1,0:T(8,128)} %get-tuple-element.535) | copy-start | bytes 6291460 | tf_op jit(solution)/shard_map/while
  395.0 15.6 %slice-start = ((s8[8388608]{0:T(1024)(128)(4,1)}), s8[4194304]{0:T(1024)(128)(4,1)S(1)}, s32[]{:S(2)}) async-start(s8[8388608]{0:T(1024)(128)(4,1)} %bitcast.205), calls=%async_computation.5 | async-start | bytes 8388608 | tf_op jit(solution)/shard_map/while
  395.0 15.6 %slice-start.1 = ((s8[8388608]{0:T(1024)(128)(4,1)}), s8[4194304]{0:T(1024)(128)(4,1)S(1)}, s32[]{:S(2)}) async-start(s8[8388608]{0:T(1024)(128)(4,1)} %bitcast.205), calls=%async_computation.6 | async-start | bytes 8388608 | tf_op jit(solution)/shard_map/while
  428.5 1.5 copy-start.10
  460.4 4.0 copy-start.5
  460.4 97.6 %all-to-all-start.3 = ((f32[32,2,8,2048]{3,2,1,0:T(8,128)}), f32[32,2,8,2048]{3,2,1,0:T(8,128)}, u32[]{:S(2)}, u32[]{:S(2)}) async-start(f32[32,2,8,2048]{3,2,1,0:T(8,128)} %get-tuple-element.238), calls=%async_computation.3 | async-start | bytes 8388608 | tf_op jit(solution)/shard_map/all_to_all | solution.py:114
  464.4 4.1 copy-start.13
  464.4 4.1 copy-start.15
  558.0 4.5 copy-start.7
  558.0 4.5 copy-start.9
  562.5 6.1 %copy-start.1 = (f32[256,512]{1,0:T(8,128)S(1)}, f32[256,512]{1,0:T(8,128)}, u32[]{:S(2)}) copy-start(f32[256,512]{1,0:T(8,128)} %param.14) | copy-start | bytes 1572868
where the time goes:
time: 573 us; the launch traced here: 569 us
  waiting for transfers between devices  266 us (46%)
  other arithmetic  172 us (30%)
  local copies, waits for them, and re-layouts  49.5 us (9%)
  blocking collectives  30 us (5%)
  matrix products  28.9 us (5%)
  starting transfers between devices  19.8 us (3%)
    all_to_all x1, waiting for transfers between devices, local(): lax.all_to_all(accum, 'ctx', split_axis=0, concat_axis=2, tiled=True)  87.2 us
    select_n x8, other arithmetic, conj_product(): real = jnp.where(zero_row, a_re * b_re, a_re * b_re + a_im * b_im)  86.5 us
    all_to_all x1, waiting for transfers between devices, local(): lax.all_to_all(carried_spec, 'ctx', split_axis=2, concat_axis=0, tiled=True)  82.4 us
    all_to_all x1, waiting for transfers between devices, local(): lax.all_to_all(gated_spec, 'ctx', split_axis=2, concat_axis=0, tiled=True)  81.6 us
    all_to_all x1, blocking collectives, local(): lax.all_to_all(lag_grads, 'ctx', split_axis=0, concat_axis=2, tiled=True)  30 us
    add x2, other arithmetic, lag_group(): accum = accum + weight * conj_product(kernel, later, zero_row)  27.9 us
    reduce_sum x8, other arithmetic, lag_group(): term = jnp.sum(weight * conj_product(gated_blk, later, zero_row), axis=0)  25.2 us
    select_n x2, other arithmetic, conj_product(): imag = jnp.where(zero_row, a_im * b_im, a_re * b_im - a_im * b_re)  25.1 us
  transfers between devices with their start and end apart: 4, of which 4 were waited for; matrix products, arithmetic and copies ran while one was open for 7% of the time, Pallas kernels for 0%

commit v1 on v0

v1 whole, which is shorter than its diff:
```python
import functools

import jax
import jax.numpy as jnp
from jax import lax
from jax.experimental import pallas as pl
from jax.experimental.pallas import tpu as pltpu
from jax.sharding import PartitionSpec as P

HALF = 128
GROUP = 8
PIECES = 2
NT = (((1,), (1,)), ((), ()))


def split_bf16(x):
    high = x.astype(jnp.bfloat16)
    low = (x - high.astype(jnp.float32)).astype(jnp.bfloat16)
    return high, low


def conv_kernel(
    ids_ref, ids_odd_ref, carried_ref, gated_ref, filter_ref,
    back_ref, lags_ref,
    even, odd, weights, accum, low_sum, high_sum,
):
    n = carried_ref.shape[0]
    rows = GROUP * n
    pairs = filter_ref.shape[1]
    lane = lax.broadcasted_iota(jnp.int32, (HALF, HALF), 1)
    place = lax.broadcasted_iota(jnp.int32, (HALF, HALF), 0)

    carried = carried_ref[:, 0]
    even[: rows] = carried.reshape(rows, HALF)
    even[rows:] = jnp.zeros((even.shape[0] - rows, HALF), jnp.float32)
    odd[...] = jnp.zeros_like(odd)
    odd[: rows - 4] = even[4:rows]

    def build(c, before):
        for side in range(2):
            row = filter_ref[0, c, :, side * HALF:(side + 1) * HALF]
            turned = pltpu.roll(
                jnp.broadcast_to(row, (HALF, HALF)), 0, 1, stride=1, stride_axis=0
            )
            tile = jnp.where(lane >= place, turned, before)
            high, low = split_bf16(tile)
            weights[c, :HALF, side * HALF:(side + 1) * HALF] = high
            weights[c, HALF:, side * HALF:(side + 1) * HALF] = low
            before = turned
        return before

    lax.fori_loop(0, pairs, build, jnp.zeros((HALF, HALF), jnp.float32))

    swap = (lane + place == HALF - 1).astype(jnp.bfloat16)
    gated_high, gated_low = split_bf16(gated_ref[:, 0].reshape(rows, HALF))
    turned_high = lax.dot_general(
        swap, gated_high, NT, preferred_element_type=jnp.float32
    ).astype(jnp.bfloat16)
    turned_low = lax.dot_general(
        swap, gated_low, NT, preferred_element_type=jnp.float32
    ).astype(jnp.bfloat16)

    accum[...] = jnp.zeros_like(accum)

    def lag_pair(c, _):
        start = pl.multiple_of(c * GROUP, GROUP)
        own = ids_ref[:rows]
        later = jnp.concatenate(
            [
                jnp.where(ids_ref[pl.ds(start, rows)] == own, even[pl.ds(start, rows)], 0.0),
                jnp.where(ids_odd_ref[pl.ds(start, rows)] == own, odd[pl.ds(start, rows)], 0.0),
            ],
            axis=1,
        )
        high, low = split_bf16(later)
        accum[...] += lax.dot_general(high, weights[c], NT, preferred_element_type=jnp.float32)
        accum[:, :HALF] += lax.dot_general(
            low, weights[c, :HALF], NT, preferred_element_type=jnp.float32
        )
        outer = (
            jnp.dot(turned_high, high, preferred_element_type=jnp.float32)
            + jnp.dot(turned_low, high, preferred_element_type=jnp.float32)
            + jnp.dot(turned_high, low, preferred_element_type=jnp.float32)
        )
        for side in range(2):
            turned = pltpu.roll(
                outer[:, side * HALF:(side + 1) * HALF], 1, 1, stride=1, stride_axis=0
            )
            inside = lane <= place
            here = jnp.where(inside, turned, 0.0).reshape(HALF // GROUP, GROUP, HALF)
            prior = jnp.where(inside, 0.0, turned).reshape(HALF // GROUP, GROUP, HALF)
            high_sum[2 * c + side] = jnp.sum(here, axis=0)
            low_sum[2 * c + side] = jnp.sum(prior, axis=0)
        return 0

    low_sum[2 * pairs] = jnp.zeros((GROUP, HALF), jnp.float32)
    lax.fori_loop(0, pairs, lag_pair, 0)
    total = accum[:, :HALF] + accum[:, HALF:]
    back_ref[:, 0] = total.reshape(n, GROUP, HALF)
    lags_ref[0] = jnp.sum(high_sum[...] + low_sum[1:], axis=1)


def convolve(ids, ids_odd, carried, gated, filters):
    n, width = carried.shape[:2]
    pairs = filters.shape[1]
    rows = GROUP * n
    padded = ids.shape[0]
    whole = pl.BlockSpec((padded, HALF), lambda f: (0, 0))
    signal = pl.BlockSpec((n, 1, GROUP, HALF), lambda f: (0, f, 0, 0))
    flops = width * 2 * pairs * 2 * rows * 256 * (256 + 128 + 192)
    return pl.pallas_call(
        conv_kernel,
        grid=(width,),
        in_specs=[
            whole, whole, signal, signal,
            pl.BlockSpec((1, pairs, 1, 2 * HALF), lambda f: (f, 0, 0, 0)),
        ],
        out_specs=[signal, pl.BlockSpec((1, 2 * pairs, HALF), lambda f: (f, 0, 0))],
        out_shape=[
            jax.ShapeDtypeStruct(carried.shape, jnp.float32),
            jax.ShapeDtypeStruct((width, 2 * pairs, HALF), jnp.float32),
        ],
        scratch_shapes=[
            pltpu.VMEM((padded, HALF), jnp.float32),
            pltpu.VMEM((padded, HALF), jnp.float32),
            pltpu.VMEM((pairs, 256, 256), jnp.bfloat16),
            pltpu.VMEM((rows, 256), jnp.float32),
            pltpu.VMEM((2 * pairs + 1, GROUP, HALF), jnp.float32),
            pltpu.VMEM((2 * pairs, GROUP, HALF), jnp.float32),
        ],
        compiler_params=pltpu.CompilerParams(vmem_limit_bytes=32 * 1024 * 1024),
        cost_estimate=pl.CostEstimate(
            flops=flops, bytes_accessed=3 * carried.size * 4, transcendentals=0
        ),
    )(ids, ids_odd, carried, gated, filters)


def local(query_branch, key_branch, value_branch, grad_output, conv_output, filters, genome_blocks):
    rows, channels = query_branch.shape
    width = filters.shape[1]
    repeats = channels // width
    blocks = lax.axis_size("ctx")
    pairs = blocks // 2
    own = width // blocks
    part = own // PIECES
    query32 = query_branch.astype(jnp.float32)
    key32 = key_branch.astype(jnp.float32)
    gated = query32 * key32
    carried = grad_output.astype(jnp.float32) * value_branch.astype(jnp.float32)
    grad_value = (grad_output.astype(jnp.float32) * conv_output.astype(jnp.float32)).astype(
        jnp.bfloat16
    )
    ends = jnp.cumsum(genome_blocks)
    block_ids = jnp.sum(
        (ends[None, :] <= jnp.arange(blocks, dtype=jnp.int32)[:, None]).astype(jnp.int32), axis=1
    )
    row_ids = jnp.repeat(block_ids, GROUP)
    pad = jnp.full((GROUP * pairs,), -1, jnp.int32)
    row_ids = jnp.concatenate([row_ids, pad])
    odd_ids = jnp.concatenate([row_ids[4:], pad[:4]])
    ids = jnp.broadcast_to(row_ids[:, None], (row_ids.shape[0], HALF))
    ids_odd = jnp.broadcast_to(odd_ids[:, None], ids.shape)

    def spread(signal):
        parts = signal.reshape(2, HALF, repeats, blocks, own).transpose(3, 4, 0, 2, 1)
        if repeats < 4:
            parts = jnp.pad(parts, ((0, 0), (0, 0), (0, 0), (0, 4 - repeats), (0, 0)))
        return parts.reshape(blocks, own, GROUP, HALF)

    def exchange(x):
        return lax.all_to_all(x, "ctx", split_axis=0, concat_axis=0, tiled=True)

    gated_parts = spread(gated)
    carried_parts = spread(carried)
    filter_parts = filters.reshape(rows, blocks, own).transpose(1, 2, 0)
    own_filters = exchange(filter_parts)[:pairs].transpose(1, 0, 2)
    backs, lags = [], []
    for piece in range(PIECES):
        chosen = slice(piece * part, (piece + 1) * part)
        back, lag = convolve(
            ids, ids_odd, exchange(carried_parts[:, chosen]), exchange(gated_parts[:, chosen]),
            own_filters[chosen, :, None],
        )
        backs.append(exchange(back))
        lags.append(lag)
    lag = jnp.concatenate(lags, axis=0).reshape(own, pairs, rows).transpose(1, 0, 2)
    lag = exchange(jnp.concatenate([lag, jnp.zeros_like(lag)], axis=0))
    back = jnp.concatenate(backs, axis=1).reshape(blocks, own, 2, 4, HALF)[:, :, :, :repeats]
    back = back.transpose(2, 4, 3, 0, 1).reshape(rows, channels)
    scaled = lag.transpose(2, 0, 1).reshape(rows, width) * (rows * blocks) ** (-0.5)
    grad_query = (back * key32).astype(jnp.bfloat16)
    grad_key = (back * query32).astype(jnp.bfloat16)
    grad_filters = lax.psum_scatter(scaled, "ch", scatter_dimension=1, tiled=True)
    return (grad_query, grad_key, grad_value, grad_filters)


def solution(mesh):
    in_specs = (
        P("ctx", "ch"),
        P("ctx", "ch"),
        P("ctx", "ch"),
        P("ctx", "ch"),
        P("ctx", "ch"),
        P("ctx", None),
        P(),
    )
    out_specs = (P("ctx", "ch"), P("ctx", "ch"), P("ctx", "ch"), P("ctx", "ch"))
    return jax.shard_map(local, mesh=mesh, in_specs=in_specs, out_specs=out_specs, check_vma=False)
```

time: 573 us -> 342 us (0.60)
  waiting for transfers between devices: 266 us -> 69 us
  other arithmetic: 172 us -> 6.04 us
  Pallas kernels: 0 us -> 133 us
  blocking collectives: 30 us -> 79.9 us
  matrix products: 28.9 us -> 0 us
  local copies, waits for them, and re-layouts: 49.5 us -> 30.8 us
    all_to_all x4 -> x5, waiting for transfers between devices: 266 us -> 69 us  [exchange(): return lax.all_to_all(x, 'ctx', split_axis=0, concat_axis=0, tiled=True)]
    pallas_call x0 -> x2, Pallas kernels: none -> 133 us  [convolve(): pl.pallas_call(conv_kernel, grid=(width,), in_specs=[whole, whole, signal...]
    select_n x12 -> x0, other arithmetic: 112 us -> none  [the longest x8 86.5 us: conj_product(): real = jnp.where(zero_row, a_re * b_re, a_re * b_re + a_im * b_im)]
    all_to_all x1 -> x3, blocking collectives: 30 us -> 79.9 us  [exchange(): return lax.all_to_all(x, 'ctx', split_axis=0, concat_axis=0, tiled=True)]
    add x4 -> x0, other arithmetic: 30.8 us -> none  [the longest x2 27.9 us: lag_group(): accum = accum + weight * conj_product(kernel, later, zero_row)]
    dot_general x10 -> x0, matrix products: 28.9 us -> none  [the longest x2 8.44 us: inverse(): jnp.dot(imag_table, spectrum[1], precision=HIGH, preferred_element_type=j...]
    reduce_sum x24 -> x0, other arithmetic: 25.4 us -> none  [the longest x8 25.2 us: lag_group(): term = jnp.sum(weight * conj_product(gated_blk, later, zero_row), axis=0)]
    all_to_all x3 -> x0, local copies, waits for them, and re-layouts: 17.5 us -> none  [the longest x1 8.13 us: local(): lax.all_to_all(gated_spec, 'ctx', split_axis=2, concat_axis=0, tiled=True)]
  transfers between devices with their start and end apart: 4 -> 5, of which waited for: 4 -> 4; matrix products, arithmetic and copies ran while one was open for 7% -> 8% of each run, Pallas kernels for 0% -> 19%
where the time goes in v1:
time: 342 us; the launch traced here: 341 us
  Pallas kernels  133 us (39%)
  blocking collectives  79.9 us (23%)
  waiting for transfers between devices  69 us (20%)
  local copies, waits for them, and re-layouts  30.8 us (9%)
  starting transfers between devices  21.5 us (6%)
  other arithmetic  6.04 us (2%)
    pallas_call x2, Pallas kernels, convolve(): pl.pallas_call(conv_kernel, grid=(width,), in_specs=[whole, whole, signal...  133 us
    all_to_all x3, blocking collectives, exchange(): return lax.all_to_all(x, 'ctx', split_axis=0, concat_axis=0, tiled=True)  79.9 us
    all_to_all x5, waiting for transfers between devices, exchange(): return lax.all_to_all(x, 'ctx', split_axis=0, concat_axis=0, tiled=True)  69 us
    all_to_all x5, starting transfers between devices, exchange(): return lax.all_to_all(x, 'ctx', split_axis=0, concat_axis=0, tiled=True)  21.5 us
    unnamed x33, local copies, waits for them, and re-layouts  13 us
  transfers between devices with their start and end apart: 5, of which 4 were waited for; matrix products, arithmetic and copies ran while one was open for 8% of the time, Pallas kernels for 19%

profile of v1, /device:TPU:0, one launch (start us, length us, event | category | flops | bytes accessed | tf_op | source)
XLA Modules:
  0.0 341.4 jit_solution(4359131481917458767)
XLA Ops:
  0.6 2.1 copy.47
  2.8 7.3 %all-to-all-start.2 = ((f32[32,16,256]{2,1,0:T(8,128)}), f32[32,16,256]{2,1,0:T(8,128)S(1)}, u32[]{:S(2)}, u32[]{:S(2)}) async-start(f32[32,16,256]{2,1,0:T(8,128)} %bitcast.7), calls=%async_computation.2 | async-start | bytes 1048576 | tf_op jit(solution)/shard_map/all_to_all | solution.py:171
  10.1 0.5 copy.44
  10.6 1.9 copy.45
  12.5 1.6 convert_multiply_fusion.1
  14.1 3.2 reshape.69
  17.4 3.4 copy.46
  20.7 1.4 fusion.3
  22.2 3.4 %all-to-all-done.2 = f32[32,16,256]{2,1,0:T(8,128)S(1)} async-done(((f32[32,16,256]{2,1,0:T(8,128)}), f32[32,16,256]{2,1,0:T(8,128)S(1)}, u32[]{:S(2)}, u32[]{:S(2)}) %all-to-all-start.2) | async-done | bytes 524320 | tf_op jit(solution)/shard_map/all_to_all | solution.py:171
  25.6 0.8 copy-done.9
  26.4 3.1 all-to-all-start.1
  29.5 3.5 %fusion = (bf16[256,2048]{1,0:T(8,128)(2,1)}, f32[256,2048]{1,0:T(8,128)S(1)}) fusion(bf16[256,2048]{1,0:T(8,128)(2,1)} %param.10, bf16[256,2048]{1,0:T(8,128)(2,1)} %param.11, bf16[256,2048]{1,0:T(8,128)(2,1)} %param.9), kind=kLoop, calls=%fused_computation.5 | loop fusion | flops 3145728 | bytes 6291456 | tf_op jit(solution)/shard_map/convert_element_type | solution.py:150
  33.0 1.8 copy.42
  34.8 2.3 reshape.67
  37.1 1.8 copy.43
  38.9 1.1 fusion.4
  40.0 15.8 %all-to-all-done.1.gated_ref = f32[32,8,8,128]{3,2,1,0:T(8,128)S(1)} async-done(((f32[32,8,8,128]{3,2,1,0:T(8,128)}), f32[32,8,8,128]{3,2,1,0:T(8,128)S(1)}, u32[]{:S(2)}, u32[]{:S(2)}) %all-to-all-start.1) | async-done | bytes 1048608 | tf_op jit(solution)/shard_map/all_to_all | solution.py:171
  55.7 29.7 %all_to_all.40.carried_ref = f32[32,8,8,128]{3,2,1,0:T(8,128)S(1)} all-to-all(f32[32,8,8,128]{3,2,1,0:T(8,128)S(1)} %get-tuple-element.28), channel_id=1, replica_groups=mesh['ctx'=32,'ch'=1] {'ctx'}, dimensions={0} | all-to-all | bytes 2097152 | tf_op jit(solution)/shard_map/all_to_all | solution.py:171
  85.4 3.6 %all-to-all-start.5 = ((f32[32,8,8,128]{3,2,1,0:T(8,128)}), f32[32,8,8,128]{3,2,1,0:T(8,128)S(1)}, u32[]{:S(2)}, u32[]{:S(2)}) async-start(f32[32,8,8,128]{3,2,1,0:T(8,128)} %get-tuple-element.27), calls=%async_computation.5 | async-start | bytes 2097152 | tf_op jit(solution)/shard_map/all_to_all | solution.py:171
  89.0 0.2 reduce-window.8
  89.2 0.1 convert_reduce_fusion
  89.4 0.1 reshape.66
  89.6 0.9 copy.61
  90.4 24.8 %all-to-all-done.5.gated_ref = f32[32,8,8,128]{3,2,1,0:T(8,128)S(1)} async-done(((f32[32,8,8,128]{3,2,1,0:T(8,128)}), f32[32,8,8,128]{3,2,1,0:T(8,128)S(1)}, u32[]{:S(2)}, u32[]{:S(2)}) %all-to-all-start.5) | async-done | bytes 1048608 | tf_op jit(solution)/shard_map/all_to_all | solution.py:171
  115.3 3.7 %all-to-all-start.4 = ((f32[32,8,8,128]{3,2,1,0:T(8,128)}), f32[32,8,8,128]{3,2,1,0:T(8,128)}, u32[]{:S(2)}, u32[]{:S(2)}) async-start(f32[32,8,8,128]{3,2,1,0:T(8,128)} %get-tuple-element.29), calls=%async_computation.4 | async-start | bytes 2097152 | tf_op jit(solution)/shard_map/all_to_all | solution.py:171
  119.0 0.1 copy.49.filter_ref
  119.2 0.7 broadcast_in_dim.14.filter_ref
  119.9 0.1 broadcast_in_dim.12.ids_odd_ref
  120.1 0.1 broadcast_in_dim.11.ids_ref
  120.2 65.8 %shard_map.102 = (f32[32,8,8,128]{3,2,1,0:T(8,128)S(1)}, f32[8,32,128]{2,1,0:T(8,128)S(1)}) custom-call(s32[384,128]{1,0:T(8,128)S(1)} %broadcast_in_dim.11.ids_ref, s32[384,128]{1,0:T(8,128)S(1)} %broadcast_in_dim.12.ids_odd_ref, f32[32,8,8,128]{3,2,1,0:T(8,128)S(1)} %all_to_all.40.carried_ref, f32[32,8,8,128]{3,2,1,0:T(8,128)S(1)} %all-to-all-done.1.gated_ref, ...), custom_call_target="tpu_custom_call" | custom-call | flops 19327352832 | bytes 3145728 | tf_op jit(solution)/shard_map/pallas_call | solution.py:111
  186.0 1.0 copy-done
  187.0 0.6 copy-done.3
  187.6 0.9 copy-done.2
  188.5 67.4 %shard_map.103 = (f32[32,8,8,128]{3,2,1,0:T(8,128)}, f32[8,32,128]{2,1,0:T(8,128)S(1)}) custom-call(s32[384,128]{1,0:T(8,128)S(1)} %broadcast_in_dim.11.ids_ref, s32[384,128]{1,0:T(8,128)S(1)} %broadcast_in_dim.12.ids_odd_ref, f32[32,8,8,128]{3,2,1,0:T(8,128)} %all-to-all-done.4.carried_ref, f32[32,8,8,128]{3,2,1,0:T(8,128)S(1)} %all-to-all-done.5.gated_ref, ...), custom_call_target="tpu_custom_call" | custom-call | flops 19327352832 | bytes 3145728 | tf_op jit(solution)/shard_map/pallas_call | solution.py:111
  256.0 0.1 reshape.74
  256.0 0.2 copy.62
  256.3 21.1 %all_to_all.41 = f32[32,16,256]{2,1,0:T(8,128)S(1)} all-to-all(f32[32,16,256]{2,1,0:T(8,128)S(1)} %concatenate.19), channel_id=1, replica_groups=mesh['ctx'=32,'ch'=1] {'ctx'}, dimensions={0} | all-to-all | bytes 1048576 | tf_op jit(solution)/shard_map/all_to_all | solution.py:171
  277.4 29.1 %all_to_all.42 = f32[32,8,8,128]{3,2,1,0:T(8,128)S(1)} all-to-all(f32[32,8,8,128]{3,2,1,0:T(8,128)S(1)} %copy-done.1), channel_id=1, replica_groups=mesh['ctx'=32,'ch'=1] {'ctx'}, dimensions={0} | all-to-all | bytes 2097152 | tf_op jit(solution)/shard_map/all_to_all | solution.py:171
  306.5 3.8 %all-to-all-start.6 = ((f32[32,8,8,128]{3,2,1,0:T(8,128)}), f32[32,8,8,128]{3,2,1,0:T(8,128)S(1)}, u32[]{:S(2)}, u32[]{:S(2)}) async-start(f32[32,8,8,128]{3,2,1,0:T(8,128)} %get-tuple-element.9), calls=%async_computation.6 | async-start | bytes 2097152 | tf_op jit(solution)/shard_map/all_to_all | solution.py:171
  310.3 1.0 copy.54
  311.3 25.0 %all-to-all-done.6 = f32[32,8,8,128]{3,2,1,0:T(8,128)S(1)} async-done(((f32[32,8,8,128]{3,2,1,0:T(8,128)}), f32[32,8,8,128]{3,2,1,0:T(8,128)S(1)}, u32[]{:S(2)}, u32[]{:S(2)}) %all-to-all-start.6) | async-done | bytes 1048608 | tf_op jit(solution)/shard_map/all_to_all | solution.py:171
  336.3 0.2 pad_maximum_fusion
  336.6 1.1 copy.50
  337.7 0.1 copy-done.6
  337.8 0.3 copy-done.8
  338.1 0.4 fusion.1
  338.5 1.4 copy.52
  339.9 1.4 copy.53
  (31 shorter events, 0.3 us)
Async XLA Ops:
  0.6 9.4 %copy-start.10 = (bf16[256,2048]{1,0:T(8,128)(2,1)S(1)}, bf16[256,2048]{1,0:T(8,128)(2,1)}, u32[]{:S(2)}) copy-start(bf16[256,2048]{1,0:T(8,128)(2,1)} %param.7) | copy-start | bytes 3145732
  2.8 22.9 %all-to-all-start.2 = ((f32[32,16,256]{2,1,0:T(8,128)}), f32[32,16,256]{2,1,0:T(8,128)S(1)}, u32[]{:S(2)}, u32[]{:S(2)}) async-start(f32[32,16,256]{2,1,0:T(8,128)} %bitcast.7), calls=%async_computation.2 | async-start | bytes 1048576 | tf_op jit(solution)/shard_map/all_to_all | solution.py:171
  10.6 3.5 %copy-start.5 = (bf16[256,2048]{0,1:T(8,128)(2,1)}, bf16[256,2048]{0,1:T(8,128)(2,1)S(1)}, u32[]{:S(2)}) copy-start(bf16[256,2048]{0,1:T(8,128)(2,1)S(1)} %copy.44) | copy-start | bytes 3145732
  12.5 1.6 copy-start.7
  25.6 0.8 copy-start.9
  26.4 29.3 %all-to-all-start.1 = ((f32[32,8,8,128]{3,2,1,0:T(8,128)}), f32[32,8,8,128]{3,2,1,0:T(8,128)S(1)}, u32[]{:S(2)}, u32[]{:S(2)}) async-start(f32[32,8,8,128]{3,2,1,0:T(8,128)} %get-tuple-element.26), calls=%async_computation.1 | async-start | bytes 2097152 | tf_op jit(solution)/shard_map/all_to_all | solution.py:171
  55.7 33.3 %copy-start.12 = (s32[4]{0:T(128)S(1)}, s32[4]{0:T(128)}, u32[]{:S(2)}) copy-start(s32[4]{0:T(128)} %param.13) | copy-start | bytes 52
  55.7 33.8 %slice-start = ((f32[32,16,256]{2,1,0:T(8,128)}), f32[16,16,256]{2,1,0:T(8,128)S(1)}, s32[]{:S(2)}) async-start(f32[32,16,256]{2,1,0:T(8,128)} %copy-done.9), calls=%async_computation.8 | async-start | bytes 524288 | tf_op jit(solution)/shard_map/slice | solution.py:176
  85.4 29.9 %all-to-all-start.5 = ((f32[32,8,8,128]{3,2,1,0:T(8,128)}), f32[32,8,8,128]{3,2,1,0:T(8,128)S(1)}, u32[]{:S(2)}, u32[]{:S(2)}) async-start(f32[32,8,8,128]{3,2,1,0:T(8,128)} %get-tuple-element.27), calls=%async_computation.5 | async-start | bytes 2097152 | tf_op jit(solution)/shard_map/all_to_all | solution.py:171
  90.4 28.6 %copy-start.11 = (f32[16,16,256]{2,0,1:T(8,128)S(1)}, f32[16,16,256]{2,0,1:T(8,128)}, u32[]{:S(2)}) copy-start(f32[16,16,256]{2,0,1:T(8,128)} %copy.61) | copy-start | bytes 786436
  115.3 72.4 %all-to-all-start.4 = ((f32[32,8,8,128]{3,2,1,0:T(8,128)}), f32[32,8,8,128]{3,2,1,0:T(8,128)}, u32[]{:S(2)}, u32[]{:S(2)}) async-start(f32[32,8,8,128]{3,2,1,0:T(8,128)} %get-tuple-element.29), calls=%async_computation.4 | async-start | bytes 2097152 | tf_op jit(solution)/shard_map/all_to_all | solution.py:171
  186.0 1.0 copy-start
  187.0 0.7 copy-start.3
  187.6 0.9 copy-start.2
  188.5 67.4 %copy-start.4 = (f32[8,32,128]{2,1,0:T(8,128)S(1)}, f32[8,32,128]{2,1,0:T(8,128)}, u32[]{:S(2)}) copy-start(f32[8,32,128]{2,1,0:T(8,128)} %copy-done.3) | copy-start | bytes 393220
  255.9 21.4 %copy-start.1 = (f32[32,8,8,128]{3,2,1,0:T(8,128)S(1)}, f32[32,8,8,128]{3,2,1,0:T(8,128)}, u32[]{:S(2)}) copy-start(f32[32,8,8,128]{3,2,1,0:T(8,128)} %copy-done) | copy-start | bytes 3145732
  306.5 29.9 %all-to-all-start.6 = ((f32[32,8,8,128]{3,2,1,0:T(8,128)}), f32[32,8,8,128]{3,2,1,0:T(8,128)S(1)}, u32[]{:S(2)}, u32[]{:S(2)}) async-start(f32[32,8,8,128]{3,2,1,0:T(8,128)} %get-tuple-element.9), calls=%async_computation.6 | async-start | bytes 2097152 | tf_op jit(solution)/shard_map/all_to_all | solution.py:171
  336.6 1.2 copy-start.6
  336.6 1.5 copy-start.8
